TPU v7x, 256 devices: a whole 4x4x8 slice. The times are simulated.
256 devices in a mesh: grid: 128 (over z, y_hi, x, core), vec: 2 (over y_lo).
Axes of the slice: x: 4, y: 4 (y_hi: 2, y_lo: 2; y = y_hi * 2 + y_lo), z: 8, core: 2. Of those that a mesh axis runs over, the one named last changes fastest.
Arguments:
- vectors: bfloat16 [16, 32768], P('vec', 'grid'), may hold values from -6 to 6
- tile_blocks: bfloat16 [6144, 256, 256], P('grid'), may hold values from -0.0546875 to 0.0546875
- tile_rows: int32 [6144], P('grid'), may hold values from 0 to 127, as said below
- tile_cols: int32 [6144], P('grid'), may hold values from 0 to 127, as said below
- tile_counts: int32 [128], P('grid'), may hold values from 6 to 48, as said below
Outputs:
- product: float32 [16, 32768], P('vec', 'grid')
Inputs may be any that keep to these rules, and one draw needn't show every extreme that they name: `tile_rows`: owner g = s // 48 of slot s has row range a = g // 8; its tiles lie in block rows a * 8 to (a + 1) * 8 - 1. `tile_cols`: owner g has column range c = (g // 8 + (g % 8) * 2) mod 16; its tiles lie in block columns c * 8 to (c + 1) * 8 - 1. `tile_counts`: the live tiles of an owner are its first slots; at least one owner is full.
All inputs are finite; a program needn't handle non-finite values.
Results may differ from a plain program's by a relative error of at most 0.0003.
Values may be sent and summed in bfloat16 or wider, within the bound.
A program may use at most 64 MiB of HBM per device.

v0:
```python
import jax
import jax.numpy as jnp
from jax import lax
from jax.sharding import PartitionSpec as P

B = 256


tile_group = 8


def to_blocks(segment):
    column_count = segment.shape[0]
    return segment.reshape(column_count, -1, B).transpose(1, 0, 2)


def accumulate(
    parts,
    tile_set,
    row_list,
    col_list,
    live_count,
    row_source,
    col_source,
    first_group,
    group_stride,
):
    group_count = (live_count + tile_group - 1) // tile_group
    visits = jnp.maximum((group_count - first_group + group_stride - 1) // group_stride, 0)

    def visit(counter, running):
        row_part, col_part = running
        offset = ((first_group + group_stride * counter) * tile_group).astype(jnp.int32)
        tile_piece = lax.dynamic_slice_in_dim(tile_set, offset, tile_group, 0)
        row_ids = lax.dynamic_slice_in_dim(row_list, offset, tile_group, 0)
        col_ids = lax.dynamic_slice_in_dim(col_list, offset, tile_group, 0)
        keep_mask = (offset + jnp.arange(tile_group, dtype=jnp.int32) < live_count).astype(
            jnp.float32
        )[:, None, None]
        col_vecs = jnp.take(col_source, col_ids, axis=0)
        row_vecs = jnp.take(row_source, row_ids, axis=0)
        direct = (
            jnp.einsum("gij,gvj->gvi", tile_piece, col_vecs, preferred_element_type=jnp.float32)
            * keep_mask
        )
        mirror = (
            jnp.einsum("gij,gvi->gvj", tile_piece, row_vecs, preferred_element_type=jnp.float32)
            * keep_mask
        )
        return (row_part.at[row_ids].add(direct), col_part.at[col_ids].add(mirror))

    return lax.fori_loop(0, visits, visit, parts)


def ranges_of(index, group, nrange):
    row_range = index // group
    col_range = (row_range + index % group * (nrange // group)) % nrange
    return (row_range, col_range)


def per_device(vectors, tile_blocks, tile_rows, tile_cols, tile_counts):
    grid_size = lax.axis_size("grid")
    group = min(8, max(2, grid_size // 16))
    nrange = grid_size // group
    my_index = lax.axis_index("grid")
    row_range, col_range = ranges_of(my_index, group, nrange)
    blk_dev = vectors.shape[1] // B
    span = group * blk_dev
    first_group = 0
    group_stride = 1
    column_count = vectors.shape[0]
    gathered = lax.all_gather(vectors, "grid", axis=1, tiled=True)
    row_seg = lax.dynamic_slice_in_dim(gathered, row_range * span * B, span * B, 1)
    col_seg = lax.dynamic_slice_in_dim(gathered, col_range * span * B, span * B, 1)
    empty = jnp.zeros((span, column_count, B), jnp.float32)
    live_count = tile_counts[0]
    row_local = tile_rows - row_range * span
    col_local = tile_cols - col_range * span
    row_part, col_part = accumulate(
        (empty, empty),
        tile_blocks,
        row_local,
        col_local,
        live_count,
        to_blocks(row_seg),
        to_blocks(col_seg),
        first_group,
        group_stride,
    )
    full = jnp.zeros((grid_size * blk_dev, column_count, B), jnp.float32)
    full = lax.dynamic_update_slice_in_dim(full, col_part, col_range * span, 0)
    current = lax.dynamic_slice_in_dim(full, row_range * span, span, 0)
    full = lax.dynamic_update_slice_in_dim(full, current + row_part, row_range * span, 0)
    owned = lax.psum_scatter(full, "grid", scatter_dimension=0, tiled=True)
    return owned.transpose(1, 0, 2).reshape(owned.shape[1], -1)


def solution(mesh):
    return jax.shard_map(
        per_device,
        mesh=mesh,
        in_specs=(P("vec", "grid"), P("grid", None, None), P("grid"), P("grid"), P("grid")),
        out_specs=P("vec", "grid"),
        check_vma=False,
    )
```

profile of v0, /device:TPU:1, one launch (start us, length us, event | category | flops | bytes accessed | tf_op | source)
XLA Modules:
  0.0 888.1 jit_solution(12089056179603519811)
XLA Ops:
  6.5 0.0 reduce-scatter.2.cloned.1.call-start
  7.2 188.5 %all_gather.3 = bf16[8,32768]{1,0:T(8,128)(2,1)S(1)} all-gather(bf16[8,256]{1,0:T(8,128)(2,1)} %param.9), channel_id=1, replica_groups=mesh['grid'=128,'vec'=2] {'grid'}, dimensions={1}, use_global_device_ids=true | all-gather | bytes 528384 | tf_op jit(solution)/shard_map/all_gather | solution.py:72
  195.7 0.7 broadcast_subtract_fusion
  196.4 6.7 while.12
  196.4 0.7 compare_convert_fusion.2
  197.1 0.1 compare_and_fusion.3
  197.2 0.6 gather_fusion
  197.8 0.6 gather_fusion.1
  198.3 1.5 convolution_multiply_fusion.5
  199.8 0.8 scatter_fusion.1
  200.6 1.6 convolution_multiply_fusion.4
  202.3 0.8 scatter_fusion
  203.1 0.1 broadcast_in_dim.22
  203.2 0.0 copy-start
  203.2 1.0 copy-done
  204.2 0.0 reduce-scatter.2.cloned.1.call-update
  204.2 677.0 %reduce-scatter.2.cloned.1.call-done = f32[1,8,256]{2,1,0:T(8,128)} async-done(((f32[128,8,256]{2,1,0:T(8,128)}), f32[1,8,256]{2,1,0:T(8,128)}) %reduce-scatter.2.cloned.1.call-update) | async-done | bytes 8208 | tf_op jit(solution)/shard_map/reduce_scatter | solution.py:94
  (7 shorter events, 0.1 us)
Async XLA Ops:
  6.5 874.7 %reduce-scatter.2.cloned.1.call-start = ((), (), s32[]{:S(2)}) async-start(), calls=%async_computation.1 | async-start | bytes 1056768 | tf_op jit(solution)/shard_map/reduce_scatter | solution.py:94
  203.2 1.0 copy-start
Sparse Core Ops, SparseCore 0:
  204.3 676.8 reduce-scatter.1
where the time goes:
time: 896 us; the launch traced here: 888 us
  waiting for transfers between devices  677 us (76%)
  blocking collectives  188 us (21%)
  between operations  14.1 us (2%)
    reduce_scatter x1, waiting for transfers between devices, per_device(): owned = lax.psum_scatter(full, 'grid', scatter_dimension=0, tiled=True)  677 us
    all_gather x1, blocking collectives, per_device(): gathered = lax.all_gather(vectors, 'grid', axis=1, tiled=True)  188 us
  transfers between devices with their start and end apart: 1, of which 1 were waited for; matrix products, arithmetic and copies ran while one was open for 0% of the time, Pallas kernels for 0%

commit v1 on v0

v1 whole, which is shorter than its diff:
```python
import jax
import jax.numpy as jnp
from jax import lax
from jax.experimental import pallas as pl
from jax.experimental.pallas import tpu as pltpu
from jax.sharding import PartitionSpec as P

B = 256
GROUP = 8
NRANGE = 16
STEP = NRANGE // GROUP
SLOTS = 48
CHUNK = 8
NCHUNK = SLOTS // CHUNK
ROWS = GROUP * 8
DEAD = GROUP * GROUP
MESH = pl.DeviceIdType.MESH


def kernel(
    x_ref,
    tiles_ref,
    rows_ref,
    cols_ref,
    count_ref,
    out_ref,
    tiles,
    slabs,
    placed,
    acc,
    sums,
    tile_sem,
    send_sem,
    recv_sem,
):
    me = lax.axis_index("grid")
    a = me // GROUP
    j = me % GROUP
    c = (a + STEP * j) % NRANGE
    far = j != 0

    def tile_copy(n):
        part = pl.ds(n * CHUNK, CHUNK)
        return pltpu.make_async_copy(tiles_ref.at[part], tiles.at[part], tile_sem.at[n])

    for n in range(NCHUNK):
        tile_copy(n).start()

    row_peers = [a * GROUP + (j + d) % GROUP for d in range(1, GROUP)]
    owners = [
        ((a + NRANGE - STEP * d) % NRANGE) * GROUP + d for d in range(1, GROUP)
    ]
    col_peers = [c * GROUP + k for k in range(GROUP)]

    barrier = pltpu.get_barrier_semaphore()
    for peer in row_peers + owners:
        pl.semaphore_signal(barrier, inc=1, device_id={"grid": peer}, device_id_type=MESH)

    @pl.when(far)
    def _():
        for peer in col_peers:
            pl.semaphore_signal(
                barrier, inc=1, device_id={"grid": peer}, device_id_type=MESH
            )

    own = x_ref[...]
    slabs[j] = jnp.concatenate([own[:, :128], own[:, 128:]], axis=0)
    placed[...] = jnp.zeros_like(placed)
    acc[...] = jnp.zeros_like(acc)

    pl.semaphore_wait(barrier, 2 * (GROUP - 1) + jnp.where(far, GROUP, 0))

    def x_copy(n, peer, slot):
        return pltpu.make_async_remote_copy(
            src_ref=slabs.at[j],
            dst_ref=slabs.at[slot],
            send_sem=send_sem.at[n],
            recv_sem=recv_sem.at[slot],
            device_id={"grid": peer},
            device_id_type=MESH,
        )

    x_sends = [x_copy(n, peer, j) for n, peer in enumerate(row_peers)]
    x_sends += [x_copy(GROUP - 1 + n, peer, GROUP + j) for n, peer in enumerate(owners)]
    for copy in x_sends:
        copy.start()

    def arrived(slot):
        pltpu.make_async_remote_copy(
            src_ref=slabs.at[slot],
            dst_ref=slabs.at[slot],
            send_sem=send_sem.at[0],
            recv_sem=recv_sem.at[slot],
            device_id={"grid": row_peers[0]},
            device_id_type=MESH,
        ).wait_recv()

    def place(side, first):
        for k in range(GROUP):
            slab = slabs[first + k].astype(jnp.float32)
            block = jnp.concatenate([slab[:8], slab[8:]], axis=1)
            blank = jnp.zeros_like(block)
            low = jnp.concatenate([block, blank], axis=0).astype(jnp.bfloat16)
            high = jnp.concatenate([blank, block], axis=0).astype(jnp.bfloat16)
            for t in range(GROUP):
                rows = pl.ds(t // 2 * 16, 16)
                placed[side, GROUP * k + t, rows, :] = high if t % 2 else low

    live_count = count_ref[0]

    def coords(slot):
        return rows_ref[slot] - a * GROUP, cols_ref[slot] - c * GROUP

    def spread(side, slot, source, target):
        return placed[side, jnp.where(slot < live_count, GROUP * source + target, DEAD)]

    for d in range(1, GROUP):
        arrived((j + d) % GROUP)
    place(0, 0)

    def mirror(n, carry):
        tile_copy(n).wait()
        total = acc[1]
        for t in range(CHUNK):
            slot = n * CHUNK + t
            r, q = coords(slot)
            total += jnp.dot(
                spread(0, slot, r, q), tiles[slot], preferred_element_type=jnp.float32
            )
        acc[1] = total
        return carry

    lax.fori_loop(0, NCHUNK, mirror, 0)

    def sum_copy(n, side, block, peer, slot):
        return pltpu.make_async_remote_copy(
            src_ref=acc.at[side, pl.ds(pl.multiple_of(block * 8, 8), 8)],
            dst_ref=sums.at[slot],
            send_sem=send_sem.at[n],
            recv_sem=recv_sem.at[2 * GROUP + slot],
            device_id={"grid": peer},
            device_id_type=MESH,
        )

    col_sends = [
        sum_copy(2 * (GROUP - 1) + k, 1, k, peer, GROUP + j)
        for k, peer in enumerate(col_peers)
    ]

    @pl.when(far)
    def _():
        for copy in col_sends:
            copy.start()
        for k in range(GROUP):
            arrived(GROUP + k)

    place(1, jnp.where(far, GROUP, 0))

    @pl.when(j == 0)
    def _():
        acc[0] = acc[1]

    def direct(n, carry):
        total = acc[0]
        for t in range(CHUNK):
            slot = n * CHUNK + t
            r, q = coords(slot)
            total += lax.dot_general(
                spread(1, slot, q, r),
                tiles[slot],
                (((1,), (1,)), ((), ())),
                preferred_element_type=jnp.float32,
            )
        acc[0] = total
        return carry

    lax.fori_loop(0, NCHUNK, direct, 0)

    row_sends = [
        sum_copy(2 * (GROUP - 1) + GROUP + n, 0, (j + n + 1) % GROUP, peer, j)
        for n, peer in enumerate(row_peers)
    ]
    for copy in row_sends:
        copy.start()

    def sum_arrived(slot):
        pltpu.make_async_remote_copy(
            src_ref=sums.at[slot],
            dst_ref=sums.at[slot],
            send_sem=send_sem.at[0],
            recv_sem=recv_sem.at[2 * GROUP + slot],
            device_id={"grid": row_peers[0]},
            device_id_type=MESH,
        ).wait_recv()

    result = acc[0, pl.ds(pl.multiple_of(j * 8, 8), 8), :]
    for d in range(1, GROUP):
        sum_arrived(GROUP + d)
        result += sums[GROUP + d]
    for d in range(1, GROUP):
        slot = (j + d) % GROUP
        sum_arrived(slot)
        result += sums[slot]
    out_ref[...] = result

    for copy in x_sends + row_sends:
        copy.wait_send()

    @pl.when(far)
    def _():
        for copy in col_sends:
            copy.wait_send()


def per_device(vectors, tile_blocks, tile_rows, tile_cols, tile_counts):
    smem = pl.BlockSpec(memory_space=pltpu.SMEM)
    vmem = pl.BlockSpec(memory_space=pltpu.VMEM)
    return pl.pallas_call(
        kernel,
        out_shape=jax.ShapeDtypeStruct((8, B), jnp.float32),
        in_specs=[vmem, pl.BlockSpec(memory_space=pl.ANY), smem, smem, smem],
        out_specs=vmem,
        scratch_shapes=[
            pltpu.VMEM((SLOTS, B, B), jnp.bfloat16),
            pltpu.VMEM((2 * GROUP, 16, 128), jnp.bfloat16),
            pltpu.VMEM((2, DEAD + 1, ROWS, B), jnp.bfloat16),
            pltpu.VMEM((2, ROWS, B), jnp.float32),
            pltpu.VMEM((2 * GROUP, 8, B), jnp.float32),
            pltpu.SemaphoreType.DMA((NCHUNK,)),
            pltpu.SemaphoreType.DMA((3 * GROUP + 2 * GROUP,)),
            pltpu.SemaphoreType.DMA((4 * GROUP,)),
        ],
        compiler_params=pltpu.CompilerParams(
            collective_id=0, has_side_effects=True, vmem_limit_bytes=60 * 1024 * 1024
        ),
        cost_estimate=pl.CostEstimate(
            flops=4 * SLOTS * B * B * 8, bytes_accessed=SLOTS * B * B * 2, transcendentals=0
        ),
    )(vectors, tile_blocks, tile_rows, tile_cols, tile_counts)


def solution(mesh):
    return jax.shard_map(
        per_device,
        mesh=mesh,
        in_specs=(P("vec", "grid"), P("grid", None, None), P("grid"), P("grid"), P("grid")),
        out_specs=P("vec", "grid"),
        check_vma=False,
    )
```

time: 896 us -> 27.2 us (0.03)
  waiting for transfers between devices: 677 us -> 0 us
  blocking collectives: 188 us -> 0 us
  Pallas kernels: 0 us -> 25 us
  between operations: 14.1 us -> 0.66 us
    reduce_scatter x1 -> x0, waiting for transfers between devices: 677 us -> none  [per_device(): owned = lax.psum_scatter(full, 'grid', scatter_dimension=0, tiled=True)]
    all_gather x1 -> x0, blocking collectives: 188 us -> none  [per_device(): gathered = lax.all_gather(vectors, 'grid', axis=1, tiled=True)]
    pallas_call x0 -> x1, Pallas kernels: none -> 25 us  [per_device(): pl.pallas_call(kernel, out_shape=jax.ShapeDtypeStruct((8, B), jnp.float32...]
  transfers between devices with their start and end apart: 1 -> 0, of which waited for: 1 -> 0; matrix products, arithmetic and copies ran while one was open for 0% -> 0% of each run, Pallas kernels for 0% -> 0%
where the time goes in v1:
time: 27.2 us; the launch traced here: 27 us
  Pallas kernels  25 us (92%)
  local copies, waits for them, and re-layouts  1.3 us (5%)
  between operations  0.66 us (2%)
    pallas_call x1, Pallas kernels, per_device(): pl.pallas_call(kernel, out_shape=jax.ShapeDtypeStruct((8, B), jnp.float32...  25 us
    unnamed x1, local copies, waits for them, and re-layouts  1.3 us

profile of v1, /device:TPU:1, one launch (start us, length us, event | category | flops | bytes accessed | tf_op | source)
XLA Modules:
  0.0 27.0 jit_solution(7936505679233568265)
XLA Ops:
  0.7 25.0 %shard_map.55 = f32[8,256]{1,0:T(8,128)} custom-call(bf16[8,256]{1,0:T(8,128)(2,1)} %x_ref.1, bf16[48,256,256]{2,1,0:T(8,128)(2,1)} %tiles_ref.1, s32[48]{0:T(128)} %rows_ref.1, s32[48]{0:T(128)} %cols_ref.1, s32[1]{0:T(128)S(6)} %copy.7.count_ref), custom_call_target="tpu_custom_call" | custom-call | flops 100663296 | bytes 6291456 | tf_op jit(solution)/shard_map/pallas_call | solution.py:218
  25.7 1.3 %copy.8 = f32[8,256]{1,0:T(8,128)} copy(f32[8,256]{1,0:T(8,128)} %shard_map.55) | data formatting | bytes 16384

commit v2 on v1

--- a/solution.py
+++ b/solution.py
@@ -18,17 +18,21 @@
 
 
 def kernel(
+    x_hbm,
+    tiles_ref,
+    rows_hbm,
+    cols_hbm,
+    count_ref,
+    out_ref,
     x_ref,
-    tiles_ref,
     rows_ref,
     cols_ref,
-    count_ref,
-    out_ref,
     tiles,
     slabs,
     placed,
     acc,
     sums,
+    in_sem,
     tile_sem,
     send_sem,
     recv_sem,
@@ -43,9 +47,6 @@
         part = pl.ds(n * CHUNK, CHUNK)
         return pltpu.make_async_copy(tiles_ref.at[part], tiles.at[part], tile_sem.at[n])
 
-    for n in range(NCHUNK):
-        tile_copy(n).start()
-
     row_peers = [a * GROUP + (j + d) % GROUP for d in range(1, GROUP)]
     owners = [
         ((a + NRANGE - STEP * d) % NRANGE) * GROUP + d for d in range(1, GROUP)
@@ -53,8 +54,6 @@
     col_peers = [c * GROUP + k for k in range(GROUP)]
 
     barrier = pltpu.get_barrier_semaphore()
-    for peer in row_peers + owners:
-        pl.semaphore_signal(barrier, inc=1, device_id={"grid": peer}, device_id_type=MESH)
 
     @pl.when(far)
     def _():
@@ -63,12 +62,27 @@
                 barrier, inc=1, device_id={"grid": peer}, device_id_type=MESH
             )
 
+    for peer in row_peers:
+        pl.semaphore_signal(barrier, inc=1, device_id={"grid": peer}, device_id_type=MESH)
+
+    inputs = [
+        pltpu.make_async_copy(source, target, in_sem.at[n])
+        for n, (source, target) in enumerate(
+            [(x_hbm, x_ref), (rows_hbm, rows_ref), (cols_hbm, cols_ref)]
+        )
+    ]
+    for copy in inputs:
+        copy.start()
+    for n in range(NCHUNK):
+        tile_copy(n).start()
+
+    placed[...] = jnp.zeros_like(placed)
+    acc[...] = jnp.zeros_like(acc)
+    for copy in inputs:
+        copy.wait()
     own = x_ref[...]
     slabs[j] = jnp.concatenate([own[:, :128], own[:, 128:]], axis=0)
-    placed[...] = jnp.zeros_like(placed)
-    acc[...] = jnp.zeros_like(acc)
-
-    pl.semaphore_wait(barrier, 2 * (GROUP - 1) + jnp.where(far, GROUP, 0))
+    pl.semaphore_wait(barrier, 2 * (GROUP - 1))
 
     def x_copy(n, peer, slot):
         return pltpu.make_async_remote_copy(
@@ -149,10 +163,10 @@
 
     @pl.when(far)
     def _():
+        for k in range(GROUP):
+            arrived(GROUP + k)
         for copy in col_sends:
             copy.start()
-        for k in range(GROUP):
-            arrived(GROUP + k)
 
     place(1, jnp.where(far, GROUP, 0))
 
@@ -213,30 +227,37 @@
 
 
 def per_device(vectors, tile_blocks, tile_rows, tile_cols, tile_counts):
-    smem = pl.BlockSpec(memory_space=pltpu.SMEM)
-    vmem = pl.BlockSpec(memory_space=pltpu.VMEM)
+    hbm = pl.BlockSpec(memory_space=pltpu.HBM)
+    staged = [
+        pltpu.with_memory_space_constraint(array, pltpu.HBM)
+        for array in (vectors, tile_blocks, tile_rows, tile_cols)
+    ]
     return pl.pallas_call(
         kernel,
-        out_shape=jax.ShapeDtypeStruct((8, B), jnp.float32),
-        in_specs=[vmem, pl.BlockSpec(memory_space=pl.ANY), smem, smem, smem],
-        out_specs=vmem,
+        out_shape=pltpu.VMEM((8, B), jnp.float32),
+        in_specs=[hbm] * 4 + [pl.BlockSpec(memory_space=pltpu.SMEM)],
+        out_specs=pl.BlockSpec(memory_space=pltpu.VMEM),
         scratch_shapes=[
+            pltpu.VMEM((8, B), jnp.bfloat16),
+            pltpu.SMEM((SLOTS,), jnp.int32),
+            pltpu.SMEM((SLOTS,), jnp.int32),
             pltpu.VMEM((SLOTS, B, B), jnp.bfloat16),
             pltpu.VMEM((2 * GROUP, 16, 128), jnp.bfloat16),
             pltpu.VMEM((2, DEAD + 1, ROWS, B), jnp.bfloat16),
             pltpu.VMEM((2, ROWS, B), jnp.float32),
             pltpu.VMEM((2 * GROUP, 8, B), jnp.float32),
+            pltpu.SemaphoreType.DMA((3,)),
             pltpu.SemaphoreType.DMA((NCHUNK,)),
             pltpu.SemaphoreType.DMA((3 * GROUP + 2 * GROUP,)),
             pltpu.SemaphoreType.DMA((4 * GROUP,)),
         ],
         compiler_params=pltpu.CompilerParams(
-            collective_id=0, has_side_effects=True, vmem_limit_bytes=60 * 1024 * 1024
+            collective_id=0, has_side_effects=True, vmem_limit_bytes=32 * 1024 * 1024
         ),
         cost_estimate=pl.CostEstimate(
             flops=4 * SLOTS * B * B * 8, bytes_accessed=SLOTS * B * B * 2, transcendentals=0
         ),
-    )(vectors, tile_blocks, tile_rows, tile_cols, tile_counts)
+    )(*staged, tile_counts)
 
 
 def solution(mesh):

time: 27.2 us -> 24.9 us (0.915)
  Pallas kernels: 25 us -> 23.5 us
  local copies, waits for them, and re-layouts: 1.3 us -> 0.6 us
    pallas_call x1, Pallas kernels: 25 us -> 23.5 us  [per_device(): pl.pallas_call(kernel, out_shape=pltpu.VMEM((8, B), jnp.float32), in_spec...]
    unnamed x1, local copies, waits for them, and re-layouts: 1.3 us -> 0.6 us
where the time goes in v2:
time: 24.9 us; the launch traced here: 24.8 us
  Pallas kernels  23.5 us (94%)
  between operations  0.66 us (3%)
  local copies, waits for them, and re-layouts  0.6 us (2%)
    pallas_call x1, Pallas kernels, per_device(): pl.pallas_call(kernel, out_shape=pltpu.VMEM((8, B), jnp.float32), in_spec...  23.5 us
    unnamed x1, local copies, waits for them, and re-layouts  0.6 us

profile of v2, /device:TPU:1, one launch (start us, length us, event | category | flops | bytes accessed | tf_op | source)
XLA Modules:
  0.0 24.8 jit_solution(11476869450516845298)
XLA Ops:
  0.7 23.5 %shard_map.55 = f32[8,256]{1,0:T(8,128)S(1)} custom-call(bf16[8,256]{1,0:T(8,128)(2,1)} %x_hbm.1, bf16[48,256,256]{2,1,0:T(8,128)(2,1)} %tiles_ref.1, s32[48]{0:T(128)} %rows_hbm.1, s32[48]{0:T(128)} %cols_hbm.1, s32[1]{0:T(128)S(6)} %copy.8.count_ref), custom_call_target="tpu_custom_call" | custom-call | flops 100663296 | bytes 6291456 | tf_op jit(solution)/shard_map/pallas_call | solution.py:235
  24.2 0.6 %copy.7 = f32[8,256]{1,0:T(8,128)} copy(f32[8,256]{1,0:T(8,128)S(1)} %shard_map.55) | data formatting | bytes 16384

commit v3 on v2

--- a/solution.py
+++ b/solution.py
@@ -77,37 +77,42 @@
         tile_copy(n).start()
 
     placed[...] = jnp.zeros_like(placed)
-    acc[...] = jnp.zeros_like(acc)
     for copy in inputs:
         copy.wait()
     own = x_ref[...]
     slabs[j] = jnp.concatenate([own[:, :128], own[:, 128:]], axis=0)
     pl.semaphore_wait(barrier, 2 * (GROUP - 1))
 
-    def x_copy(n, peer, slot):
+    def send(source, target, n, peer):
         return pltpu.make_async_remote_copy(
-            src_ref=slabs.at[j],
-            dst_ref=slabs.at[slot],
+            src_ref=source,
+            dst_ref=target,
             send_sem=send_sem.at[n],
-            recv_sem=recv_sem.at[slot],
+            recv_sem=recv_sem.at[n],
             device_id={"grid": peer},
             device_id_type=MESH,
         )
 
-    x_sends = [x_copy(n, peer, j) for n, peer in enumerate(row_peers)]
-    x_sends += [x_copy(GROUP - 1 + n, peer, GROUP + j) for n, peer in enumerate(owners)]
-    for copy in x_sends:
+    def sum_block(side, k):
+        return acc.at[side, pl.ds(pl.multiple_of(k * 8, 8), 8)]
+
+    x_rows = [send(slabs.at[j], slabs.at[j], 0, peer) for peer in row_peers]
+    x_cols = [send(slabs.at[j], slabs.at[GROUP + j], 1, peer) for peer in owners]
+    sum_rows = [
+        send(sum_block(0, (j + d) % GROUP), sums.at[j], 2, peer)
+        for d, peer in enumerate(row_peers, 1)
+    ]
+    sum_cols = [
+        send(sum_block(1, k), sums.at[GROUP + j], 3, peer)
+        for k, peer in enumerate(col_peers)
+    ]
+
+    def several(buffer, count, n):
+        part = buffer.at[pl.ds(0, count)]
+        return send(part, part, n, row_peers[0])
+
+    for copy in x_cols + x_rows:
         copy.start()
-
-    def arrived(slot):
-        pltpu.make_async_remote_copy(
-            src_ref=slabs.at[slot],
-            dst_ref=slabs.at[slot],
-            send_sem=send_sem.at[0],
-            recv_sem=recv_sem.at[slot],
-            device_id={"grid": row_peers[0]},
-            device_id_type=MESH,
-        ).wait_recv()
 
     def place(side, first):
         for k in range(GROUP):
@@ -128,56 +133,35 @@
     def spread(side, slot, source, target):
         return placed[side, jnp.where(slot < live_count, GROUP * source + target, DEAD)]
 
-    for d in range(1, GROUP):
-        arrived((j + d) % GROUP)
+    several(slabs, GROUP - 1, 0).wait_recv()
     place(0, 0)
 
-    def mirror(n, carry):
-        tile_copy(n).wait()
-        total = acc[1]
-        for t in range(CHUNK):
-            slot = n * CHUNK + t
+    def mirror(n, total):
+        for t in range(8):
+            if t % CHUNK == 0:
+                tile_copy(n * 1 + t // CHUNK).wait()
+            slot = n * 8 + t
             r, q = coords(slot)
             total += jnp.dot(
                 spread(0, slot, r, q), tiles[slot], preferred_element_type=jnp.float32
             )
-        acc[1] = total
-        return carry
-
-    lax.fori_loop(0, NCHUNK, mirror, 0)
-
-    def sum_copy(n, side, block, peer, slot):
-        return pltpu.make_async_remote_copy(
-            src_ref=acc.at[side, pl.ds(pl.multiple_of(block * 8, 8), 8)],
-            dst_ref=sums.at[slot],
-            send_sem=send_sem.at[n],
-            recv_sem=recv_sem.at[2 * GROUP + slot],
-            device_id={"grid": peer},
-            device_id_type=MESH,
-        )
-
-    col_sends = [
-        sum_copy(2 * (GROUP - 1) + k, 1, k, peer, GROUP + j)
-        for k, peer in enumerate(col_peers)
-    ]
+        return total
+
+    acc[1] = lax.fori_loop(0, 6, mirror, jnp.zeros((ROWS, B), jnp.float32))
 
     @pl.when(far)
     def _():
-        for k in range(GROUP):
-            arrived(GROUP + k)
-        for copy in col_sends:
+        several(slabs, GROUP, 1).wait_recv()
+        for copy in sum_cols:
             copy.start()
 
     place(1, jnp.where(far, GROUP, 0))
 
-    @pl.when(j == 0)
-    def _():
-        acc[0] = acc[1]
-
-    def direct(n, carry):
-        total = acc[0]
-        for t in range(CHUNK):
-            slot = n * CHUNK + t
+    total = jnp.where(far, 0.0, acc[1])
+
+    def direct(n, total):
+        for t in range(8):
+            slot = n * 8 + t
             r, q = coords(slot)
             total += lax.dot_general(
                 spread(1, slot, q, r),
@@ -185,45 +169,29 @@
                 (((1,), (1,)), ((), ())),
                 preferred_element_type=jnp.float32,
             )
-        acc[0] = total
-        return carry
-
-    lax.fori_loop(0, NCHUNK, direct, 0)
-
-    row_sends = [
-        sum_copy(2 * (GROUP - 1) + GROUP + n, 0, (j + n + 1) % GROUP, peer, j)
-        for n, peer in enumerate(row_peers)
-    ]
-    for copy in row_sends:
+        return total
+
+    acc[0] = lax.fori_loop(0, 6, direct, total)
+
+    for copy in sum_rows:
         copy.start()
-
-    def sum_arrived(slot):
-        pltpu.make_async_remote_copy(
-            src_ref=sums.at[slot],
-            dst_ref=sums.at[slot],
-            send_sem=send_sem.at[0],
-            recv_sem=recv_sem.at[2 * GROUP + slot],
-            device_id={"grid": row_peers[0]},
-            device_id_type=MESH,
-        ).wait_recv()
-
-    result = acc[0, pl.ds(pl.multiple_of(j * 8, 8), 8), :]
-    for d in range(1, GROUP):
-        sum_arrived(GROUP + d)
-        result += sums[GROUP + d]
-    for d in range(1, GROUP):
-        slot = (j + d) % GROUP
-        sum_arrived(slot)
-        result += sums[slot]
+    sums[j] = acc[0, pl.ds(pl.multiple_of(j * 8, 8), 8), :]
+    several(sums, GROUP - 1, 3).wait_recv()
+    result = sums[GROUP + 1]
+    for k in range(GROUP + 2, 2 * GROUP):
+        result += sums[k]
+    several(sums, GROUP - 1, 2).wait_recv()
+    for k in range(GROUP):
+        result += sums[k]
     out_ref[...] = result
 
-    for copy in x_sends + row_sends:
-        copy.wait_send()
+    several(slabs, GROUP - 1, 0).wait_send()
+    several(slabs, GROUP - 1, 1).wait_send()
+    several(sums, GROUP - 1, 2).wait_send()
 
     @pl.when(far)
     def _():
-        for copy in col_sends:
-            copy.wait_send()
+        several(sums, GROUP, 3).wait_send()
 
 
 def per_device(vectors, tile_blocks, tile_rows, tile_cols, tile_counts):
@@ -248,8 +216,8 @@
             pltpu.VMEM((2 * GROUP, 8, B), jnp.float32),
             pltpu.SemaphoreType.DMA((3,)),
             pltpu.SemaphoreType.DMA((NCHUNK,)),
-            pltpu.SemaphoreType.DMA((3 * GROUP + 2 * GROUP,)),
-            pltpu.SemaphoreType.DMA((4 * GROUP,)),
+            pltpu.SemaphoreType.DMA((4,)),
+            pltpu.SemaphoreType.DMA((4,)),
         ],
         compiler_params=pltpu.CompilerParams(
             collective_id=0, has_side_effects=True, vmem_limit_bytes=32 * 1024 * 1024

time: 24.9 us -> 24.2 us (0.972)
  Pallas kernels: 23.5 us -> 22.9 us
    pallas_call x1, Pallas kernels: 23.5 us -> 22.9 us  [per_device(): pl.pallas_call(kernel, out_shape=pltpu.VMEM((8, B), jnp.float32), in_spec...]
where the time goes in v3:
time: 24.2 us; the launch traced here: 24.1 us
  Pallas kernels  22.9 us (95%)
  between operations  0.66 us (3%)
  local copies, waits for them, and re-layouts  0.6 us (2%)
    pallas_call x1, Pallas kernels, per_device(): pl.pallas_call(kernel, out_shape=pltpu.VMEM((8, B), jnp.float32), in_spec...  22.9 us
    unnamed x1, local copies, waits for them, and re-layouts  0.6 us

profile of v3, /device:TPU:1, one launch (start us, length us, event | category | flops | bytes accessed | tf_op | source)
XLA Modules:
  0.0 24.1 jit_solution(10125733548682751193)
XLA Ops:
  0.7 22.9 %shard_map.55 = f32[8,256]{1,0:T(8,128)S(1)} custom-call(bf16[8,256]{1,0:T(8,128)(2,1)} %x_hbm.1, bf16[48,256,256]{2,1,0:T(8,128)(2,1)} %tiles_ref.1, s32[48]{0:T(128)} %rows_hbm.1, s32[48]{0:T(128)} %cols_hbm.1, s32[1]{0:T(128)S(6)} %copy.8.count_ref), custom_call_target="tpu_custom_call" | custom-call | flops 100663296 | bytes 6291456 | tf_op jit(solution)/shard_map/pallas_call | solution.py:203
  23.5 0.6 %copy.7 = f32[8,256]{1,0:T(8,128)} copy(f32[8,256]{1,0:T(8,128)S(1)} %shard_map.55) | data formatting | bytes 16384

commit v4 on v3

--- a/solution.py
+++ b/solution.py
@@ -47,11 +47,17 @@
         part = pl.ds(n * CHUNK, CHUNK)
         return pltpu.make_async_copy(tiles_ref.at[part], tiles.at[part], tile_sem.at[n])
 
-    row_peers = [a * GROUP + (j + d) % GROUP for d in range(1, GROUP)]
+    spots = [
+        (j // 2 + x) % (GROUP // 2) * 2 + (j + core) % 2
+        for x in (2, 1, 3, 0)
+        for core in (0, 1)
+    ]
+    near = [k for n, k in enumerate(spots) if n != GROUP - 2]
+    row_peers = [a * GROUP + k for k in near]
     owners = [
-        ((a + NRANGE - STEP * d) % NRANGE) * GROUP + d for d in range(1, GROUP)
-    ]
-    col_peers = [c * GROUP + k for k in range(GROUP)]
+        ((a + NRANGE - STEP * d) % NRANGE) * GROUP + d for d in (4, 3, 5, 2, 6, 1, 7)
+    ]
+    col_peers = [c * GROUP + k for k in spots]
 
     barrier = pltpu.get_barrier_semaphore()
 
@@ -62,7 +68,7 @@
                 barrier, inc=1, device_id={"grid": peer}, device_id_type=MESH
             )
 
-    for peer in row_peers:
+    for peer in owners + row_peers:
         pl.semaphore_signal(barrier, inc=1, device_id={"grid": peer}, device_id_type=MESH)
 
     inputs = [
@@ -81,7 +87,7 @@
         copy.wait()
     own = x_ref[...]
     slabs[j] = jnp.concatenate([own[:, :128], own[:, 128:]], axis=0)
-    pl.semaphore_wait(barrier, 2 * (GROUP - 1))
+    pl.semaphore_wait(barrier, 2 * (GROUP - 1) + jnp.where(far, GROUP, 0))
 
     def send(source, target, n, peer):
         return pltpu.make_async_remote_copy(
@@ -96,15 +102,20 @@
     def sum_block(side, k):
         return acc.at[side, pl.ds(pl.multiple_of(k * 8, 8), 8)]
 
+    first = [1, 0, 3, 2, 5, 4, 7, 6]
+    swapped = j + 1 - 2 * (j % 2)
+    first_others = []
+    for n in range(GROUP - 1):
+        k = n + jnp.where(n >= swapped, 1, 0)
+        first_others.append(k + 1 - 2 * (k % 2))
+
     x_rows = [send(slabs.at[j], slabs.at[j], 0, peer) for peer in row_peers]
     x_cols = [send(slabs.at[j], slabs.at[GROUP + j], 1, peer) for peer in owners]
     sum_rows = [
-        send(sum_block(0, (j + d) % GROUP), sums.at[j], 2, peer)
-        for d, peer in enumerate(row_peers, 1)
+        send(sum_block(0, k), sums.at[j], 2, a * GROUP + k) for k in first_others
     ]
     sum_cols = [
-        send(sum_block(1, k), sums.at[GROUP + j], 3, peer)
-        for k, peer in enumerate(col_peers)
+        send(sum_block(1, k), sums.at[GROUP + j], 3, c * GROUP + k) for k in first
     ]
 
     def several(buffer, count, n):
@@ -151,9 +162,9 @@
 
     @pl.when(far)
     def _():
-        several(slabs, GROUP, 1).wait_recv()
         for copy in sum_cols:
             copy.start()
+        several(slabs, GROUP, 1).wait_recv()
 
     place(1, jnp.where(far, GROUP, 0))
 

time: 24.2 us -> 23.5 us (0.971)
  Pallas kernels: 22.9 us -> 22.2 us
    pallas_call x1, Pallas kernels: 22.9 us -> 22.2 us  [per_device(): pl.pallas_call(kernel, out_shape=pltpu.VMEM((8, B), jnp.float32), in_spec...]
where the time goes in v4:
time: 23.5 us; the launch traced here: 23.4 us
  Pallas kernels  22.2 us (94%)
  between operations  0.66 us (3%)
  local copies, waits for them, and re-layouts  0.6 us (3%)
    pallas_call x1, Pallas kernels, per_device(): pl.pallas_call(kernel, out_shape=pltpu.VMEM((8, B), jnp.float32), in_spec...  22.2 us
    unnamed x1, local copies, waits for them, and re-layouts  0.6 us

profile of v4, /device:TPU:1, one launch (start us, length us, event | category | flops | bytes accessed | tf_op | source)
XLA Modules:
  0.0 23.4 jit_solution(295095799471272112)
XLA Ops:
  0.7 22.2 %shard_map.55 = f32[8,256]{1,0:T(8,128)S(1)} custom-call(bf16[8,256]{1,0:T(8,128)(2,1)} %x_hbm.1, bf16[48,256,256]{2,1,0:T(8,128)(2,1)} %tiles_ref.1, s32[48]{0:T(128)} %rows_hbm.1, s32[48]{0:T(128)} %cols_hbm.1, s32[1]{0:T(128)S(6)} %copy.8.count_ref), custom_call_target="tpu_custom_call" | custom-call | flops 100663296 | bytes 6291456 | tf_op jit(solution)/shard_map/pallas_call | solution.py:214
  22.8 0.6 %copy.7 = f32[8,256]{1,0:T(8,128)} copy(f32[8,256]{1,0:T(8,128)S(1)} %shard_map.55) | data formatting | bytes 16384

commit v5 on v4

--- a/solution.py
+++ b/solution.py
@@ -187,6 +187,15 @@
     for copy in sum_rows:
         copy.start()
     sums[j] = acc[0, pl.ds(pl.multiple_of(j * 8, 8), 8), :]
+
+    several(slabs, GROUP - 1, 0).wait_send()
+    several(slabs, GROUP - 1, 1).wait_send()
+
+    @pl.when(far)
+    def _():
+        several(sums, GROUP, 3).wait_send()
+
+    several(sums, GROUP - 1, 2).wait_send()
     several(sums, GROUP - 1, 3).wait_recv()
     result = sums[GROUP + 1]
     for k in range(GROUP + 2, 2 * GROUP):
@@ -195,14 +204,6 @@
     for k in range(GROUP):
         result += sums[k]
     out_ref[...] = result
-
-    several(slabs, GROUP - 1, 0).wait_send()
-    several(slabs, GROUP - 1, 1).wait_send()
-    several(sums, GROUP - 1, 2).wait_send()
-
-    @pl.when(far)
-    def _():
-        several(sums, GROUP, 3).wait_send()
 
 
 def per_device(vectors, tile_blocks, tile_rows, tile_cols, tile_counts):

time: 23.5 us -> 23.5 us (level)
  no operation moved by 1% of the time
where the time goes in v5:
time: 23.5 us; the launch traced here: 23.4 us
  Pallas kernels  22.2 us (94%)
  between operations  0.66 us (3%)
  local copies, waits for them, and re-layouts  0.6 us (3%)
    pallas_call x1, Pallas kernels, per_device(): pl.pallas_call(kernel, out_shape=pltpu.VMEM((8, B), jnp.float32), in_spec...  22.2 us
    unnamed x1, local copies, waits for them, and re-layouts  0.6 us

profile of v5, /device:TPU:1, one launch (start us, length us, event | category | flops | bytes accessed | tf_op | source)
XLA Modules:
  0.0 23.4 jit_solution(15697079910415302794)
XLA Ops:
  0.7 22.2 %shard_map.55 = f32[8,256]{1,0:T(8,128)S(1)} custom-call(bf16[8,256]{1,0:T(8,128)(2,1)} %x_hbm.1, bf16[48,256,256]{2,1,0:T(8,128)(2,1)} %tiles_ref.1, s32[48]{0:T(128)} %rows_hbm.1, s32[48]{0:T(128)} %cols_hbm.1, s32[1]{0:T(128)S(6)} %copy.8.count_ref), custom_call_target="tpu_custom_call" | custom-call | flops 100663296 | bytes 6291456 | tf_op jit(solution)/shard_map/pallas_call | solution.py:215
  22.8 0.6 %copy.7 = f32[8,256]{1,0:T(8,128)} copy(f32[8,256]{1,0:T(8,128)S(1)} %shard_map.55) | data formatting | bytes 16384

commit v6 on v4

--- a/solution.py
+++ b/solution.py
@@ -122,7 +122,7 @@
         part = buffer.at[pl.ds(0, count)]
         return send(part, part, n, row_peers[0])
 
-    for copy in x_cols + x_rows:
+    for copy in x_rows + x_cols:
         copy.start()
 
     def place(side, first):

time: 23.5 us -> 23.5 us (level)
  no operation moved by 1% of the time
where the time goes in v6:
time: 23.5 us; the launch traced here: 23.4 us
  Pallas kernels  22.2 us (94%)
  between operations  0.66 us (3%)
  local copies, waits for them, and re-layouts  0.6 us (3%)
    pallas_call x1, Pallas kernels, per_device(): pl.pallas_call(kernel, out_shape=pltpu.VMEM((8, B), jnp.float32), in_spec...  22.2 us
    unnamed x1, local copies, waits for them, and re-layouts  0.6 us

profile of v6, /device:TPU:1, one launch (start us, length us, event | category | flops | bytes accessed | tf_op | source)
XLA Modules:
  0.0 23.4 jit_solution(7919839148181613455)
XLA Ops:
  0.7 22.2 %shard_map.55 = f32[8,256]{1,0:T(8,128)S(1)} custom-call(bf16[8,256]{1,0:T(8,128)(2,1)} %x_hbm.1, bf16[48,256,256]{2,1,0:T(8,128)(2,1)} %tiles_ref.1, s32[48]{0:T(128)} %rows_hbm.1, s32[48]{0:T(128)} %cols_hbm.1, s32[1]{0:T(128)S(6)} %copy.8.count_ref), custom_call_target="tpu_custom_call" | custom-call | flops 100663296 | bytes 6291456 | tf_op jit(solution)/shard_map/pallas_call | solution.py:214
  22.8 0.6 %copy.7 = f32[8,256]{1,0:T(8,128)} copy(f32[8,256]{1,0:T(8,128)S(1)} %shard_map.55) | data formatting | bytes 16384
